TPU v7x, 512 devices: a whole 4x8x8 slice. The times are simulated.
512 devices in a mesh: team: 64 (over z_hi, y, core), loop: 8 (over z_lo, x).
Axes of the slice: x: 4, y: 8, z: 8 (z_hi: 4, z_lo: 2; z = z_hi * 2 + z_lo), core: 2. Of those that a mesh axis runs over, the one named last changes fastest.
Arguments:
- src_pos: float32 [3, 262144], P(None, ('team', 'loop')), may hold values from -6 to 6
- src_vel: float32 [3, 262144], P(None, ('team', 'loop')), may hold values from -5 to 5
- src_mass: float32 [262144], P(('team', 'loop')), may hold values from 0.2 to 5
- old_accel: float32 [6, 8192], P(None, ('team', 'loop')), may hold values from -6 to 6
- active_index: int32 [8192], P(('team', 'loop')), may hold values from 0 to 511, as said below
- active_level: int32 [8192], P(('team', 'loop')), may hold values from 0 to 3
- tile_id: int32 [8192], P(('team', 'loop')), may hold values from 0 to 511
- tile_offset: int32 [2, 8192], P(None, ('team', 'loop')), may hold values from 16 to 112
Outputs:
- new_state: float32 [12, 8192], P(None, ('team', 'loop'))
- image: float32 [2, 512, 128, 128], P(None, ('team', 'loop'))
Inputs may be any that keep to these rules, and one draw needn't show every extreme that they name: `active_index`: the 16 entries of one device are distinct rows of that device's 512 source stars.
All inputs are finite; a program needn't handle non-finite values.
Results may differ from a plain program's by a relative error of at most 0.0027.
Values sent between devices are 32-bit elements; how exact they have to be, the bound alone decides.
A program may use at most 64 MiB of HBM per device.

v0:
```python
import math
import jax
import jax.numpy as jnp
from jax import lax
from jax.sharding import PartitionSpec as P

TILE_DEV = 1
TILE_W = 128


def from_behind(block, axis, distance):
    devices = range(lax.axis_size(axis))
    route = [((i - distance) % len(devices), i) for i in devices]
    return lax.ppermute(block, axis, route)


def pair_terms(tgt_pos, tgt_vel, blk_pos, blk_vel, blk_mass, gravity, soften_sq):
    separation = blk_pos[:, None, :] - tgt_pos[:, :, None]
    rel_vel = blk_vel[:, None, :] - tgt_vel[:, :, None]
    dist_sq = jnp.sum(separation * separation, axis=0) + soften_sq
    inverse = lax.rsqrt(dist_sq)
    inverse_sq = inverse * inverse
    strength = (gravity * blk_mass)[None, :] * inverse * inverse_sq
    radial = 3.0 * jnp.sum(separation * rel_vel, axis=0) * inverse_sq
    acceleration = jnp.sum(strength[None] * separation, axis=2)
    jerk_sum = jnp.sum(strength[None] * (rel_vel - radial[None] * separation), axis=2)
    return jnp.concatenate([acceleration, jerk_sum], axis=0)


def correct(targets, force, old_accel, level_float):
    step_len = jnp.exp2(-level_float)
    accel_gap = old_accel[0:3] - force[0:3]
    first_term = -6.0 * accel_gap - step_len * (4.0 * old_accel[3:6] + 2.0 * force[3:6])
    second = 12.0 * accel_gap + 6.0 * step_len * (old_accel[3:6] + force[3:6])
    new_pos = targets[0:3] + step_len * step_len * (first_term / 24.0 + second / 120.0)
    new_vel = targets[3:6] + step_len * (first_term / 6.0 + second / 24.0)
    return jnp.concatenate([new_pos, new_vel, force], axis=0)


def ingredients(new_state, star_mass, offsets, width):
    swing_cells = width / 16.0
    centre_y = offsets[0] + swing_cells * jnp.tanh(new_state[1])
    centre_x = offsets[1] + swing_cells * jnp.tanh(new_state[0])
    return jnp.stack([star_mass, star_mass * new_state[5] * new_state[5], centre_y, centre_x])


def kernel_rows(centre, width):
    cell_mid = jnp.arange(width, dtype=jnp.float32) + 0.5
    scaled = (cell_mid[None, :] - centre[:, None]) / (width / 40.0)
    return jnp.exp(-0.5 * scaled * scaled)


def block_forces(targets, source, gravity, soften_sq):
    source_len = source.shape[1]
    block_len = math.gcd(source_len, 512)
    blocks = source.reshape(7, source_len // block_len, block_len).transpose(1, 0, 2)

    def add_block(running, block_now):
        return (
            running
            + pair_terms(
                targets[0:3],
                targets[3:6],
                block_now[0:3],
                block_now[3:6],
                block_now[6],
                gravity,
                soften_sq,
            ),
            None,
        )

    return lax.scan(add_block, jnp.zeros((6, targets.shape[1]), jnp.float32), blocks)[0]


def shards(src_pos, src_vel, src_mass, old_accel, active_index, active_level, tile_id, tile_offset):
    total_stars = src_pos.shape[1] * lax.axis_size("team") * lax.axis_size("loop")
    gravity = 1.0 / total_stars
    soften_sq = float(total_stars) ** (-2.0 / 3.0)
    own_records = jnp.concatenate(
        [jnp.take(src_pos, active_index, axis=1), jnp.take(src_vel, active_index, axis=1)], axis=0
    )
    own_mass = jnp.take(src_mass, active_index, axis=0)
    source = jnp.concatenate([src_pos, src_vel, src_mass[None]], axis=0)
    owned_tiles = lax.axis_index(("team", "loop")) * TILE_DEV + jnp.arange(
        TILE_DEV, dtype=jnp.int32
    )
    empty_image = jnp.zeros((2, TILE_DEV, TILE_W, TILE_W), jnp.float32)
    targets = lax.all_gather(own_records, "team", axis=1, tiled=True)
    total_force = block_forces(targets, source, gravity, soften_sq)
    moving = source
    for turn in range(lax.axis_size("loop") - 1):
        moving = from_behind(moving, "loop", 1)
        total_force = total_force + block_forces(targets, moving, gravity, soften_sq)
    own_force = lax.psum_scatter(total_force, "team", scatter_dimension=1, tiled=True)
    new_state = correct(own_records, own_force, old_accel, active_level.astype(jnp.float32))
    deposit_parts = ingredients(new_state, own_mass, tile_offset.astype(jnp.float32), TILE_W)
    deposit_deposit_parts = lax.all_gather(deposit_parts, ("team", "loop"), axis=1, tiled=True)
    tile_rows = lax.all_gather(tile_id[None], ("team", "loop"), axis=1, tiled=True)
    row_count = deposit_deposit_parts.shape[1]
    star_block = math.gcd(row_count, 256)
    order = jnp.argsort(tile_rows[0], stable=True)
    sorted_tiles = jnp.take(tile_rows[0], order, axis=0)
    sorted_parts = jnp.take(deposit_deposit_parts, order, axis=1)
    low_row = jnp.sum((sorted_tiles < owned_tiles[0]).astype(jnp.int32))
    high_row = jnp.sum((sorted_tiles <= owned_tiles[TILE_DEV - 1]).astype(jnp.int32))
    first_block = low_row // star_block
    end_block = (high_row + star_block - 1) // star_block

    def add_stars(block_idx, running):
        first_row = block_idx * star_block
        part_block = lax.dynamic_slice_in_dim(sorted_parts, first_row, star_block, 1)
        tile_block = lax.dynamic_slice_in_dim(sorted_tiles, first_row, star_block, 0)
        tile_mask = (tile_block[None, :] == owned_tiles[:, None]).astype(jnp.float32)
        weighted = part_block[0:2, :, None] * kernel_rows(part_block[2], TILE_W)[None]
        left_rows = (weighted[:, None] * tile_mask[None, :, :, None]).astype(jnp.bfloat16)
        right_rows = kernel_rows(part_block[3], TILE_W).astype(jnp.bfloat16)
        return running + jnp.einsum(
            "ltsy,sx->ltyx", left_rows, right_rows, preferred_element_type=jnp.float32
        )

    image = lax.fori_loop(first_block, end_block, add_stars, empty_image)
    return (new_state, image)


def solution(mesh):
    return jax.shard_map(
        shards,
        mesh=mesh,
        in_specs=(
            P(None, ("team", "loop")),
            P(None, ("team", "loop")),
            P(("team", "loop")),
            P(None, ("team", "loop")),
            P(("team", "loop")),
            P(("team", "loop")),
            P(("team", "loop")),
            P(None, ("team", "loop")),
        ),
        out_specs=(P(None, ("team", "loop")), P(None, ("team", "loop"), None, None)),
        check_vma=False,
    )
```

profile of v0, /device:TPU:2, one launch (start us, length us, event | category | flops | bytes accessed | tf_op | source)
XLA Modules:
  0.0 1785.6 jit_solution(9198500476613658640)
XLA Ops:
  8.0 3.4 collective-permute-start
  15.7 89.0 %all-gather.1 = f32[64,16,6]{1,2,0:T(8,128)S(1)} all-gather(f32[1,16,6]{1,2,0:T(8,128)S(1)} %maximum_bitcast_fusion), channel_id=1, replica_groups=mesh['team'=64,'loop'=8] {'team'}, dimensions={0}, use_global_device_ids=true | all-gather | bytes 24960 | tf_op jit(solution)/shard_map/all_gather | solution.py:89
  105.7 95.0 %all-reduce = s32[8192]{0:T(1024)S(1)} all-reduce(s32[8192]{0:T(1024)S(1)} %dynamic-update-slice), channel_id=2, replica_groups=mesh['team'=64,'loop'=8] {'team','loop'}, use_global_device_ids=true, to_apply=%add | all-reduce | flops 8192 | bytes 65536
  200.8 6.8 sort.17
  207.6 45.5 %gather_fusion = s32[8192]{0:T(1024)S(1)} fusion(s32[8192]{0:T(1024)S(1)} %all-reduce, s32[8192]{0:T(1024)S(1)} %fusion.63), kind=kCustom, calls=%fused_computation.2 | custom fusion | bytes 98304 | tf_op jit(solution)/shard_map/jit(_take)/gather | solution.py:103
  253.8 2.1 collective-permute-start.1
  255.9 3.5 collective-permute-done.1
  259.4 1.8 fusion.39
  261.2 2.1 collective-permute-start.2
  264.0 4.3 collective-permute-done.2
  268.3 1.9 collective-permute-start.3
  270.3 5.8 collective-permute-done.3
  276.1 8.1 fusion.40
  284.2 1.6 multiply_multiply_fusion.7
  285.8 2.1 collective-permute-start.4
  288.0 2.6 multiply_multiply_fusion.14
  290.6 3.0 collective-permute-done.4
  293.6 1.9 collective-permute-start.5
  295.5 5.8 collective-permute-done.5
  301.3 1.9 collective-permute-start.6
  303.3 5.8 collective-permute-done.6
  309.1 14.1 fusion.37
  323.2 3.0 multiply_multiply_fusion.8
  326.1 3.0 fusion.43
  332.7 10.1 fusion.34
  342.9 1.0 copy.97
  347.7 139.5 %reduce-scatter.4.cloned.1.call-done = f32[16,6]{1,0:T(8,128)} async-done(((f32[1024,6]{1,0:T(8,128)}), f32[16,6]{1,0:T(8,128)}) %reduce-scatter.4.cloned.1.call-update) | async-done | bytes 400
  488.7 1244.0 %all-gather.2 = f32[512,16,4]{1,2,0:T(4,128)S(1)} all-gather(f32[1,16,4]{1,2,0:T(4,128)S(1)} %maximum_bitcast_fusion.1), channel_id=1, replica_groups=mesh['team'=64,'loop'=8] {'team','loop'}, dimensions={0}, use_global_device_ids=true | all-gather | bytes 131328 | tf_op jit(solution)/shard_map/all_gather | solution.py:98
  1732.6 4.5 copy.94
  1737.1 29.9 %gather_fusion.2 = f32[8192,4]{1,0:T(8,128)} fusion(f32[4,8192]{0,1:T(8,128)} %bitcast.52, s32[8192]{0:T(1024)S(1)} %fusion.63), kind=kCustom, calls=%fused_computation.4 | custom fusion | bytes 294912 | tf_op jit(solution)/shard_map/jit(_take)/gather | solution.py:104
  1767.0 7.4 select_bitcast_fusion
  1774.5 2.8 copy.95
  (82 shorter events, 15.4 us)
Async XLA Ops:
  7.2 480.0 %reduce-scatter.4.cloned.1.call-start = ((), (), s32[]{:S(2)}) async-start(), calls=%async_computation.1 | async-start | bytes 532480
  8.0 245.8 %collective-permute-start = (f32[7,512]{1,0:T(8,128)S(1)}, f32[7,512]{1,0:T(8,128)S(1)}, u32[]{:S(2)}, u32[]{:S(2)}) collective-permute-start(f32[7,512]{1,0:T(8,128)S(1)} %pad_maximum_fusion), channel_id=1, source_target_pairs={{7,0},{0,1},{1,2},{2,3},{3,4},{4,5},{5,6},{6,7},{15,8},{8,9},{9,10... | collective-permute-start | bytes 43016 | tf_op jit(solution)/shard_map/ppermute | solution.py:14
  207.6 46.2 %copy-start = (f32[512]{0:T(512)S(1)}, f32[512]{0:T(512)}, u32[]{:S(2)}) copy-start(f32[512]{0:T(512)} %param.14) | copy-start | bytes 6148
  253.8 5.6 collective-permute-start.1
  261.2 7.1 collective-permute-start.2
  263.3 12.8 copy-start.3
  263.3 12.8 copy-start.4
  268.3 7.7 collective-permute-start.3
  285.8 7.7 collective-permute-start.4
  293.6 7.7 collective-permute-start.5
  301.3 7.7 collective-permute-start.6
  330.5 1.6 copy-start.1
  330.5 2.2 copy-start.2
  332.7 11.3 copy-start.9
  332.7 14.9 copy-start.7
  332.7 155.2 %copy-start.6 = (f32[6,16]{1,0:T(8,128)S(1)}, f32[6,16]{1,0:T(8,128)}, u32[]{:S(2)}) copy-start(f32[6,16]{1,0:T(8,128)} %param.15) | copy-start | bytes 1156
  332.7 155.3 %copy-start.8 = (s32[16]{0:T(128)S(1)}, s32[16]{0:T(128)}, u32[]{:S(2)}) copy-start(s32[16]{0:T(128)} %param.16) | copy-start | bytes 196
  1778.1 0.7 copy-start.5
Sparse Core Ops, SparseCore 0:
  344.1 143.0 reduce-scatter.3
where the time goes:
time: 1790 us
  blocking collectives  1430 us (80%)
  waiting for transfers between devices  168 us (9%)
  local copies, waits for them, and re-layouts  91.7 us (5%)
  other arithmetic  65 us (4%)
    all_gather x1, blocking collectives, shards(): lax.all_gather(deposit_parts, ('team', 'loop'), axis=1, tiled=True)  1240 us
    unnamed x2, waiting for transfers between devices  140 us
    unnamed x1, blocking collectives  95 us
    all_gather x1, blocking collectives, shards(): targets = lax.all_gather(own_records, 'team', axis=1, tiled=True)  89 us
    gather x1, local copies, waits for them, and re-layouts, shards(): sorted_tiles = jnp.take(tile_rows[0], order, axis=0)  45.5 us
  transfers between devices with their start and end apart: 8, of which 7 were waited for; matrix products, arithmetic and copies ran while one was open for 3% of the time, Pallas kernels for 0%

commit v1 on v0

--- a/solution.py
+++ b/solution.py
@@ -86,7 +86,9 @@
         TILE_DEV, dtype=jnp.int32
     )
     empty_image = jnp.zeros((2, TILE_DEV, TILE_W, TILE_W), jnp.float32)
-    targets = lax.all_gather(own_records, "team", axis=1, tiled=True)
+    targets = jnp.concatenate(
+        lax.all_to_all(jnp.stack([own_records] * lax.axis_size("team")), "team", 0, 0), axis=1
+    )
     total_force = block_forces(targets, source, gravity, soften_sq)
     moving = source
     for turn in range(lax.axis_size("loop") - 1):

time: 1790 us -> 1720 us (0.961)
  blocking collectives: 1430 us -> 1340 us
  starting transfers between devices: 15.4 us -> 33.4 us
    all_gather x1 -> x0, blocking collectives: 89 us -> none  [shards(): targets = lax.all_gather(own_records, 'team', axis=1, tiled=True)]
  transfers between devices with their start and end apart: 8 -> 9, of which waited for: 7 -> 7; matrix products, arithmetic and copies ran while one was open for 3% -> 4% of each run, Pallas kernels for 0% -> 0%
where the time goes in v1:
time: 1720 us
  blocking collectives  1340 us (78%)
  waiting for transfers between devices  167 us (10%)
  local copies, waits for them, and re-layouts  92.5 us (5%)
  other arithmetic  68.9 us (4%)
  starting transfers between devices  33.4 us (2%)
  between operations  17.5 us (1%)
    all_gather x1, blocking collectives, shards(): lax.all_gather(deposit_parts, ('team', 'loop'), axis=1, tiled=True)  1240 us
    unnamed x2, waiting for transfers between devices  144 us
    unnamed x1, blocking collectives  98.5 us
    gather x1, local copies, waits for them, and re-layouts, shards(): sorted_tiles = jnp.take(tile_rows[0], order, axis=0)  45.5 us
    reduce_sum x4, other arithmetic, pair_terms(): acceleration = jnp.sum(strength[None] * separation, axis=2)  37.5 us
  transfers between devices with their start and end apart: 9, of which 7 were waited for; matrix products, arithmetic and copies ran while one was open for 4% of the time, Pallas kernels for 0%

profile of v1, /device:TPU:2, one launch (start us, length us, event | category | flops | bytes accessed | tf_op | source)
XLA Modules:
  0.0 1722.6 jit_solution(12391863718480742441)
XLA Ops:
  12.2 16.6 all-to-all-start
  29.6 3.4 collective-permute-start
  33.9 98.5 %all-reduce = s32[8192]{0:T(1024)S(1)} all-reduce(s32[8192]{0:T(1024)S(1)} %dynamic-update-slice), channel_id=2, replica_groups=mesh['team'=64,'loop'=8] {'team','loop'}, use_global_device_ids=true, to_apply=%add | all-reduce | flops 8192 | bytes 65536
  132.4 6.8 sort.17
  139.2 45.5 %gather_fusion = s32[8192]{0:T(1024)S(1)} fusion(s32[8192]{0:T(1024)S(1)} %all-reduce, s32[8192]{0:T(1024)S(1)} %fusion.63), kind=kCustom, calls=%fused_computation.2 | custom fusion | bytes 98304 | tf_op jit(solution)/shard_map/jit(_take)/gather | solution.py:105
  185.4 1.9 collective-permute-start.1
  187.4 3.7 collective-permute-done.1
  191.1 1.9 collective-permute-start.2
  193.0 4.3 collective-permute-done.2
  197.2 2.1 collective-permute-start.3
  199.7 1.8 fusion.39
  202.2 2.8 collective-permute-done.3
  205.0 10.2 fusion.40
  215.2 3.6 multiply_multiply_fusion.7
  218.8 2.0 collective-permute-start.4
  220.8 2.6 multiply_multiply_fusion.14
  223.5 3.1 collective-permute-done.4
  226.5 3.2 collective-permute-start.5
  229.8 4.4 collective-permute-done.5
  234.2 2.1 collective-permute-start.6
  236.4 5.6 collective-permute-done.6
  242.0 14.9 fusion.37
  256.9 3.0 multiply_multiply_fusion.8
  259.9 2.6 fusion.43
  266.0 9.7 fusion.34
  275.8 1.0 copy.100
  280.5 143.7 %reduce-scatter.4.cloned.1.call-done = f32[16,6]{1,0:T(8,128)} async-done(((f32[1024,6]{1,0:T(8,128)}), f32[16,6]{1,0:T(8,128)}) %reduce-scatter.4.cloned.1.call-update) | async-done | bytes 400
  425.6 1244.0 %all-gather.1 = f32[512,16,4]{1,2,0:T(4,128)S(1)} all-gather(f32[1,16,4]{1,2,0:T(4,128)S(1)} %maximum_bitcast_fusion), channel_id=1, replica_groups=mesh['team'=64,'loop'=8] {'team','loop'}, dimensions={0}, use_global_device_ids=true | all-gather | bytes 131328 | tf_op jit(solution)/shard_map/all_gather | solution.py:100
  1669.7 4.5 copy.97
  1674.2 29.9 %gather_fusion.2 = f32[8192,4]{1,0:T(8,128)} fusion(f32[4,8192]{0,1:T(8,128)} %bitcast.46, s32[8192]{0:T(1024)S(1)} %fusion.63), kind=kCustom, calls=%fused_computation.4 | custom fusion | bytes 294912 | tf_op jit(solution)/shard_map/jit(_take)/gather | solution.py:106
  1704.1 7.5 select_bitcast_fusion
  1711.5 2.8 copy.98
  (86 shorter events, 16.1 us)
Async XLA Ops:
  12.2 187.2 %all-to-all-start = ((f32[64,6,16]{2,1,0:T(8,128)}), f32[64,6,16]{2,1,0:T(8,128)S(1)}, u32[]{:S(2)}, u32[]{:S(2)}) async-start(f32[64,6,16]{2,1,0:T(8,128)} %stack.4), calls=%async_computation | async-start | bytes 524288 | tf_op jit(solution)/shard_map/all_to_all | solution.py:90
  28.8 395.4 %reduce-scatter.4.cloned.1.call-start = ((), (), s32[]{:S(2)}) async-start(), calls=%async_computation.2 | async-start | bytes 532480
  29.6 155.8 %collective-permute-start = (f32[7,512]{1,0:T(8,128)S(1)}, f32[7,512]{1,0:T(8,128)S(1)}, u32[]{:S(2)}, u32[]{:S(2)}) collective-permute-start(f32[7,512]{1,0:T(8,128)S(1)} %pad_maximum_fusion), channel_id=1, source_target_pairs={{7,0},{0,1},{1,2},{2,3},{3,4},{4,5},{5,6},{6,7},{15,8},{8,9},{9,10... | collective-permute-start | bytes 43016 | tf_op jit(solution)/shard_map/ppermute | solution.py:14
  139.2 46.2 %copy-start = (f32[512]{0:T(512)S(1)}, f32[512]{0:T(512)}, u32[]{:S(2)}) copy-start(f32[512]{0:T(512)} %param.14) | copy-start | bytes 6148
  185.4 5.6 collective-permute-start.1
  191.1 6.2 collective-permute-start.2
  197.2 7.7 collective-permute-start.3
  201.5 3.5 copy-start.3
  201.5 3.5 copy-start.4
  218.8 7.7 collective-permute-start.4
  226.5 7.7 collective-permute-start.5
  234.2 7.7 collective-permute-start.6
  263.7 1.6 copy-start.1
  263.8 2.2 copy-start.2
  266.0 10.8 copy-start.9
  266.0 14.5 copy-start.7
  266.0 159.0 %copy-start.6 = (f32[6,16]{1,0:T(8,128)S(1)}, f32[6,16]{1,0:T(8,128)}, u32[]{:S(2)}) copy-start(f32[6,16]{1,0:T(8,128)} %param.15) | copy-start | bytes 1156
  266.0 159.0 %copy-start.8 = (s32[16]{0:T(128)S(1)}, s32[16]{0:T(128)}, u32[]{:S(2)}) copy-start(s32[16]{0:T(128)} %param.16) | copy-start | bytes 196
  1715.1 0.7 copy-start.5
Sparse Core Ops, SparseCore 0:
  276.9 147.1 reduce-scatter.3
